TPU v7x, 32 devices: a whole 2x2x4 slice. The times are simulated.
32 devices in a mesh: slab: 16 (over z, y, x), col: 2 (over core).
Axes of the slice: x: 2, y: 2, z: 4, core: 2. Of those that a mesh axis runs over, the one named last changes fastest.
Arguments:
- diagonal_tiles: float32 [64, 128, 128], P(('slab', 'col')), as said below
- lower_tiles: float32 [64, 128, 128], P(('slab', 'col')), may hold values from -0.109375 to 0.109375
- upper_tiles: float32 [64, 128, 128], P(('slab', 'col')), may hold values from -0.109375 to 0.109375
- tile_pattern: int32 [64, 2], P(('slab', 'col')), may hold values 0 or 1
- interface_ids: int32 [8192], P('slab'), may hold values from 0 to 4095
- coupling_values: float32 [8192], P('slab'), may hold values from -1.5 to 1.5
- warm_start: float32 [8192, 512], P('slab', 'col'), may hold values from -6 to 6
- boundary_stiffness: float32 [512, 512], P('slab', 'col'), may hold values from -6 to 6
Outputs:
- constraint_modes: float32 [8192, 512], P('slab', 'col')
- reduced_stiffness: float32 [512, 512], P('slab', 'col')
Inputs may be any that keep to these rules, and one draw needn't show every extreme that they name: `interface_ids`: values of 512 or more mark rows coupled to no interface column. `diagonal_tiles`: every tile is symmetric positive definite.
All inputs are finite; a program needn't handle non-finite values. No bound on the sum of `tile_pattern` on one device may be relied on, other than what follows from the above.
Results may differ from a plain program's by a relative error of at most 0.00017.
Values sent between devices are 32-bit elements; how exact they have to be, the bound alone decides.
A program may use at most 64 MiB of HBM per device.

v0:
```python
import jax
import jax.numpy as jnp
from jax import lax
from jax.sharding import PartitionSpec as P

IFACE = 512
TILE = 128
SWEEPS = 2


def extended_2(value, sides, width):
    for axis, dim in sides:
        count, length = (lax.axis_size(axis), value.shape[dim])
        up = [(i, (i + 1) % count) for i in range(count - 1)]
        down = [(j, i) for i, j in up]
        last = lax.slice_in_dim(value, length - width, length, axis=dim)
        initial = lax.slice_in_dim(value, 0, width, axis=dim)
        before = lax.ppermute(last, axis, up)
        after = lax.ppermute(initial, axis, down)
        value = jnp.concatenate([before, value, after], axis=dim)
    return value


def tile_inverse(factors):
    count = factors.shape[0]
    size = factors.shape[1]
    identity = jnp.broadcast_to(jnp.eye(size, dtype=jnp.float32), (count, size, size))
    inner = lax.linalg.triangular_solve(factors, identity, left_side=True, lower=True)
    return lax.linalg.triangular_solve(factors, inner, left_side=True, lower=True, transpose_a=True)


def sweep(inverses, lower_masked, upper_masked, right_side, extended, blocks_here):
    width = extended.shape[1]
    below = extended[: blocks_here * TILE].reshape(blocks_here, TILE, width)
    above = extended[2 * TILE :].reshape(blocks_here, TILE, width)
    residual = right_side - jnp.einsum(
        "bij,bjc->bic", lower_masked, below, precision=lax.Precision.HIGHEST
    )
    residual = residual - jnp.einsum(
        "bij,bjc->bic", upper_masked, above, precision=lax.Precision.HIGHEST
    )
    updated = jnp.einsum("bij,bjc->bic", inverses, residual, precision=lax.Precision.HIGHEST)
    return updated.reshape(blocks_here * TILE, width)


def build_rhs(ids, values, width, blocks_here):
    targets = jnp.arange(width, dtype=jnp.int32)
    dense = jnp.where(ids[:, None] == targets[None, :], -values[:, None], jnp.float32(0.0))
    return dense.reshape(blocks_here, TILE, width)


def on_device(
    diagonal_tiles,
    lower_tiles,
    upper_tiles,
    tile_pattern,
    interface_ids,
    coupling_values,
    warm_start,
    boundary_stiffness,
):
    present = tile_pattern.astype(jnp.float32)
    lower_masked = lower_tiles * present[:, 0][:, None, None]
    upper_masked = upper_tiles * present[:, 1][:, None, None]
    inverses = tile_inverse(jnp.linalg.cholesky(diagonal_tiles))
    blocks_here = diagonal_tiles.shape[0]
    rows_here = blocks_here * TILE
    first_row = lax.axis_index("col") * rows_here
    own_ids = lax.dynamic_slice_in_dim(interface_ids, first_row, rows_here)
    own_values = lax.dynamic_slice_in_dim(coupling_values, first_row, rows_here)
    width = warm_start.shape[1] * lax.axis_size("col")
    right_side = build_rhs(own_ids, own_values, width, blocks_here)
    block_modes = lax.all_to_all(warm_start, "col", split_axis=0, concat_axis=1, tiled=True)
    for step in range(SWEEPS):
        extended = extended_2(block_modes, ((("slab", "col"), 0),), TILE)
        block_modes = sweep(inverses, lower_masked, upper_masked, right_side, extended, blocks_here)
    modes = lax.all_to_all(block_modes, "col", split_axis=1, concat_axis=0, tiled=True)
    weight = jnp.where(interface_ids < IFACE, coupling_values, jnp.float32(0.0))
    owned = boundary_stiffness.shape[0]
    targets = lax.iota(jnp.int32, IFACE)
    select = jnp.where(
        targets[:, None] == interface_ids[None, :], weight[None, :], jnp.float32(0.0)
    )
    total = lax.psum(
        jnp.dot(select, modes, precision=lax.Precision.HIGHEST, preferred_element_type=jnp.float32),
        "slab",
    )
    share = lax.dynamic_slice_in_dim(total, lax.axis_index("slab") * owned, owned)
    return (modes, boundary_stiffness + share)


def solution(mesh):
    placed = (
        P(("slab", "col"), None, None),
        P(("slab", "col"), None, None),
        P(("slab", "col"), None, None),
        P(("slab", "col"), None),
        P("slab"),
        P("slab"),
        P("slab", "col"),
        P("slab", "col"),
    )
    return jax.shard_map(
        on_device,
        mesh=mesh,
        in_specs=placed,
        out_specs=(P("slab", "col"), P("slab", "col")),
        check_vma=False,
    )
```

profile of v0, /device:TPU:0, one launch (start us, length us, event | category | flops | bytes accessed | tf_op | source)
XLA Modules:
  0.0 209.4 jit_solution(1945439417830244461)
XLA Ops:
  7.2 5.2 %all_to_all.38 = f32[2,256,256]{2,1,0:T(8,128)S(1)} all-to-all(f32[2,256,256]{2,1,0:T(8,128)} %bitcast.52), channel_id=1, replica_groups=mesh['slab'=16,'col'=2] {'col'}, dimensions={0} | all-to-all | bytes 1048576 | tf_op jit(solution)/shard_map/all_to_all | solution.py:73
  12.5 0.1 copy.32
  12.6 2.1 collective-permute-start
  14.7 0.1 copy.35
  14.8 1.3 collective-permute-start.1
  16.2 0.7 copy-done.6
  16.9 0.2 slice_reduce_fusion
  17.2 23.5 %custom-call.9 = f32[2,128,128]{2,1,0:T(8,128)S(1)} custom-call(f32[2,128,128]{2,1,0:T(8,128)S(1)} %fusion.10), custom_call_target="Cholesky" | custom-call | tf_op jit(solution)/shard_map/jit(cholesky)/cholesky | solution.py:65
  40.9 19.7 %custom-call.10 = f32[2,1,128,128]{2,3,1,0:T(8,128)S(1)} custom-call(f32[2,1,128,128]{3,2,1,0:T(8,128)S(1)} %select_bitcast_fusion), custom_call_target="InvertDiagBlocksLowerTriangular" | custom-call | tf_op jit(solution)/shard_map/triangular_solve | solution.py:29
  60.7 0.4 fusion.8
  61.1 0.3 copy-done.4
  61.4 0.2 copy.33
  61.6 0.3 fusion.6
  62.0 0.2 copy.34
  62.2 0.2 copy.36
  62.4 0.7 copy-done.1
  63.1 0.7 convolution_subtract_fusion.2
  63.8 0.2 copy-done
  64.0 0.6 convolution_subtract_fusion.1
  64.7 0.6 fusion.24
  65.3 5.5 %collective-permute-start.2 = (f32[128,512]{1,0:T(8,128)S(1)}, f32[128,512]{1,0:T(8,128)S(1)}, u32[]{:S(2)}, u32[]{:S(2)}) collective-permute-start(f32[128,512]{1,0:T(8,128)S(1)} %get-tuple-element.6), channel_id=1, source_target_pairs={{0,1},{1,2},{2,3},{3,4},{4,5},{5,6},{6,7},{7,8},{8,9},{9,10},{10,1... | collective-permute-start | bytes 786440 | tf_op jit(solution)/shard_map/ppermute | solution.py:18
  70.8 1.5 collective-permute-start.3
  72.3 3.2 %collective-permute-done.3 = f32[128,512]{1,0:T(8,128)S(1)} collective-permute-done((f32[128,512]{1,0:T(8,128)S(1)}, f32[128,512]{1,0:T(8,128)S(1)}, u32[]{:S(2)}, u32[]{:S(2)}) %collective-permute-start.3) | collective-permute-done | bytes 262176 | tf_op jit(solution)/shard_map/ppermute | solution.py:19
  75.5 0.6 fusion.11
  76.1 0.7 fusion
  76.8 0.6 fusion.25
  77.4 0.3 all_to_all.32
  77.8 9.4 %all_to_all.39 = f32[256,2,256]{2,0,1:T(8,128)S(1)} all-to-all(f32[256,2,256]{2,0,1:T(8,128)S(1)} %copy.37), channel_id=1, replica_groups=mesh['slab'=16,'col'=2] {'col'}, dimensions={1} | all-to-all | bytes 1048576 | tf_op jit(solution)/shard_map/all_to_all | solution.py:77
  87.2 1.8 fusion.1
  89.0 111.3 %all-reduce.2.cloned.1.call-done = f32[512,256]{1,0:T(8,128)} async-done(((f32[512,256]{1,0:T(8,128)}), f32[512,256]{1,0:T(8,128)}) %all-reduce.2.cloned.1.call-update) | async-done | bytes 524304 | tf_op jit(solution)/shard_map/psum | solution.py:84
  200.3 1.4 dynamic-slice_add_fusion
  201.7 0.8 copy.41
  (32 shorter events, 0.9 us)
Async XLA Ops:
  7.2 193.2 %all-reduce.2.cloned.1.call-start = ((), (), s32[]{:S(2)}) async-start(), calls=%async_computation.2 | async-start | bytes 1048576 | tf_op jit(solution)/shard_map/psum | solution.py:84
  12.6 49.3 %collective-permute-start = (f32[128,512]{0,1:T(8,128)S(1)}, f32[128,512]{0,1:T(8,128)S(1)}, u32[]{:S(2)}, u32[]{:S(2)}) collective-permute-start(f32[128,512]{0,1:T(8,128)S(1)} %bitcast.53), channel_id=1, source_target_pairs={{0,1},{1,2},{2,3},{3,4},{4,5},{5,6},{6,7},{7,8},{8,9},{9,10},{10,1... | collective-permute-start | bytes 786440 | tf_op jit(solution)/shard_map/ppermute | solution.py:18
  14.7 2.4 %copy-start.2 = (f32[2,128,128]{2,1,0:T(8,128)S(1)}, f32[2,128,128]{2,1,0:T(8,128)}, u32[]{:S(2)}) copy-start(f32[2,128,128]{2,1,0:T(8,128)} %param.8) | copy-start | bytes 393220
  14.8 47.1 %collective-permute-start.1 = (f32[128,512]{0,1:T(8,128)S(1)}, f32[128,512]{0,1:T(8,128)S(1)}, u32[]{:S(2)}, u32[]{:S(2)}) collective-permute-start(f32[128,512]{0,1:T(8,128)S(1)} %bitcast.54), channel_id=1, source_target_pairs={{1,0},{2,1},{3,2},{4,3},{5,4},{6,5},{7,6},{8,7},{9,8},{10,9},{11,1... | collective-permute-start | bytes 786440 | tf_op jit(solution)/shard_map/ppermute | solution.py:19
  16.2 0.7 copy-start.6
  40.9 19.7 %copy-start.5 = (s32[512]{0:T(512)S(1)}, s32[512]{0:T(512)}, u32[]{:S(2)}) copy-start(s32[512]{0:T(512)} %param.12) | copy-start | bytes 6148
  60.7 0.7 copy-start.4
  62.2 0.9 copy-start.1
  63.1 0.9 copy-start
  65.3 7.0 %collective-permute-start.2 = (f32[128,512]{1,0:T(8,128)S(1)}, f32[128,512]{1,0:T(8,128)S(1)}, u32[]{:S(2)}, u32[]{:S(2)}) collective-permute-start(f32[128,512]{1,0:T(8,128)S(1)} %get-tuple-element.6), channel_id=1, source_target_pairs={{0,1},{1,2},{2,3},{3,4},{4,5},{5,6},{6,7},{7,8},{8,9},{9,10},{10,1... | collective-permute-start | bytes 786440 | tf_op jit(solution)/shard_map/ppermute | solution.py:18
  70.8 4.7 %collective-permute-start.3 = (f32[128,512]{1,0:T(8,128)S(1)}, f32[128,512]{1,0:T(8,128)S(1)}, u32[]{:S(2)}, u32[]{:S(2)}) collective-permute-start(f32[128,512]{1,0:T(8,128)S(1)} %get-tuple-element.7), channel_id=1, source_target_pairs={{1,0},{2,1},{3,2},{4,3},{5,4},{6,5},{7,6},{8,7},{9,8},{10,9},{11,1... | collective-permute-start | bytes 786440 | tf_op jit(solution)/shard_map/ppermute | solution.py:19
  89.0 111.3 %copy-start.3 = (f32[32,256]{1,0:T(8,128)S(1)}, f32[32,256]{1,0:T(8,128)}, u32[]{:S(2)}) copy-start(f32[32,256]{1,0:T(8,128)} %param.15) | copy-start | bytes 98308
Sparse Core Ops, SparseCore 0:
  89.2 111.1 all-reduce.1
where the time goes:
time: 210 us; the launch traced here: 209 us
  waiting for transfers between devices  114 us (54%)
  other arithmetic  45.1 us (21%)
  blocking collectives  14.6 us (7%)
  between operations  14.3 us (7%)
  starting transfers between devices  10.3 us (5%)
  matrix products  6.22 us (3%)
  local copies, waits for them, and re-layouts  4.35 us (2%)
    psum x1, waiting for transfers between devices, on_device(): lax.psum(jnp.dot(select, modes, precision=lax.Precision.HIGHEST, preferre...  111 us
    another operation x4, other arithmetic, on_device(): inverses = tile_inverse(jnp.linalg.cholesky(diagonal_tiles))  23.6 us
    another operation x3, other arithmetic, tile_inverse(): lax.linalg.triangular_solve(factors, inner, left_side=True, lower=True, t...  19.8 us
    all_to_all x1, blocking collectives, on_device(): lax.all_to_all(block_modes, 'col', split_axis=1, concat_axis=0, tiled=True)  9.37 us
    ppermute x2, starting transfers between devices, extended_2(): before = lax.ppermute(last, axis, up)  7.51 us
    all_to_all x1, blocking collectives, on_device(): lax.all_to_all(warm_start, 'col', split_axis=0, concat_axis=1, tiled=True)  5.23 us
  transfers between devices with their start and end apart: 5, of which 2 were waited for; matrix products, arithmetic and copies ran while one was open for 21% of the time, Pallas kernels for 0%

commit v1 on v0

v1 whole, which is shorter than its diff:
```python
import functools

import jax
import jax.numpy as jnp
from jax import lax
from jax.experimental import pallas as pl
from jax.experimental.pallas import tpu as pltpu
from jax.sharding import PartitionSpec as P

IFACE = 512
TILE = 128
SWEEPS = 2
NEAR = 4
HIGH = lax.Precision.HIGHEST
MESH = pl.DeviceIdType.MESH


def tile_inverse(factors):
    count = factors.shape[0]
    size = factors.shape[1]
    identity = jnp.broadcast_to(jnp.eye(size, dtype=jnp.float32), (count, size, size))
    inner = lax.linalg.triangular_solve(factors, identity, left_side=True, lower=True)
    return lax.linalg.triangular_solve(factors, inner, left_side=True, lower=True, transpose_a=True)


def dot(a, b):
    return jnp.dot(a, b, precision=HIGH, preferred_element_type=jnp.float32)


def body(
    slabs,
    reduce_here,
    pattern_ref,
    inv_in,
    lower_ref,
    upper_ref,
    ids_ref,
    values_ref,
    warm_ref,
    boundary_ref,
    modes_ref,
    reduced_ref,
    lu,
    inv,
    halo,
    mid,
    parts,
    near_in,
    far_out,
    far_in,
    pair_send,
    pair_recv,
    halo_send,
    halo_recv,
    near_send,
    near_recv,
    far_send,
    far_recv,
):
    slab, col = lax.axis_index("slab"), lax.axis_index("col")
    here = lower_ref.shape[0]
    blocks = 2 * here
    width = warm_ref.shape[1]
    other = (slab, 1 - col)
    far = slabs // NEAR
    owned = IFACE // slabs
    hi, lo = slab // NEAR, lax.rem(slab, NEAR)
    near_ids = [(hi * NEAR + lax.rem(lo + k, NEAR), col) for k in range(1, NEAR)]
    far_ids = [(lax.rem(hi + k, far) * NEAR + lo, col) for k in range(1, far)]
    is_first, is_last = slab == 0, slab == slabs - 1

    barrier = pltpu.get_barrier_semaphore()
    steps = range(1, slabs) if reduce_here else (1, slabs - 1)
    partners = [other] + [(lax.rem(slab + k, slabs), col) for k in steps]
    for partner in partners:
        pl.semaphore_signal(barrier, inc=1, device_id=partner, device_id_type=MESH)

    for b in range(here):
        at = col * here + b
        lu[at, :, :TILE] = lower_ref[b] * pattern_ref[b, 0].astype(jnp.float32)
        lu[at, :, TILE:] = upper_ref[b] * pattern_ref[b, 1].astype(jnp.float32)
        inv[at] = inv_in[b]

    pl.semaphore_wait(barrier, len(partners))

    def halos(step, first_block, last_block):
        down = pltpu.make_async_remote_copy(
            src_ref=first_block,
            dst_ref=halo.at[2 * step + 1],
            send_sem=halo_send.at[2 * step],
            recv_sem=halo_recv.at[2 * step + 1],
            device_id=(slab - 1, col),
            device_id_type=MESH,
        )
        up = pltpu.make_async_remote_copy(
            src_ref=last_block,
            dst_ref=halo.at[2 * step],
            send_sem=halo_send.at[2 * step + 1],
            recv_sem=halo_recv.at[2 * step],
            device_id=(slab + 1, col),
            device_id_type=MESH,
        )
        return down, up

    def start_halos(copies):
        down, up = copies

        @pl.when(jnp.logical_not(is_first))
        def _():
            down.start()

        @pl.when(jnp.logical_not(is_last))
        def _():
            up.start()

    def wait_halos(step, copies):
        down, up = copies

        @pl.when(jnp.logical_not(is_first))
        def _():
            down.wait_send()
            up.wait_recv()

        @pl.when(is_first)
        def _():
            halo[2 * step] = jnp.zeros((TILE, width), jnp.float32)

        @pl.when(jnp.logical_not(is_last))
        def _():
            up.wait_send()
            down.wait_recv()

        @pl.when(is_last)
        def _():
            halo[2 * step + 1] = jnp.zeros((TILE, width), jnp.float32)

    def pair(ref, which):
        mine = ref.at[pl.ds(col * here, here)]
        return pltpu.make_async_remote_copy(
            src_ref=mine,
            dst_ref=mine,
            send_sem=pair_send.at[which],
            recv_sem=pair_recv.at[which],
            device_id=other,
            device_id_type=MESH,
        )

    warm_halos = halos(0, warm_ref.at[pl.ds(0, TILE)], warm_ref.at[pl.ds((blocks - 1) * TILE, TILE)])
    start_halos(warm_halos)
    tiles = pair(lu, 0)
    tiles.start()
    inverses = pair(inv, 1)
    inverses.start()

    rows = blocks * TILE
    ids_row = jnp.minimum(ids_ref[...], IFACE).astype(jnp.float32)
    values_row = values_ref[...]
    ids_col = jnp.broadcast_to(ids_row, (8, rows)).T[:, :1].astype(jnp.int32)
    values_col = jnp.broadcast_to(values_row, (8, rows)).T[:, :1]
    columns = lax.broadcasted_iota(jnp.int32, (TILE, width), 1) + col * width

    def right_side(b):
        part = slice(b * TILE, (b + 1) * TILE)
        return jnp.where(ids_col[part] == columns, -values_col[part], 0.0)

    tiles.wait()
    inverses.wait()

    def update(b, below, above):
        both = jnp.concatenate([below, above], axis=0)
        return dot(inv[b], right_side(b) - dot(lu[b], both))

    def old(ref, step, b):
        if b < 0:
            return halo[2 * step]
        if b >= blocks:
            return halo[2 * step + 1]
        return ref[b * TILE : (b + 1) * TILE, :]

    wait_halos(0, warm_halos)
    mid_halos = halos(1, mid.at[pl.ds(0, TILE)], mid.at[pl.ds((blocks - 1) * TILE, TILE)])
    order = [0, blocks - 1] + list(range(1, blocks - 1))
    for n, b in enumerate(order):
        mid[b * TILE : (b + 1) * TILE, :] = update(b, old(warm_ref, 0, b - 1), old(warm_ref, 0, b + 1))
        if n == 1:
            start_halos(mid_halos)
    for n, b in enumerate(order[2:] + order[:2]):
        if n == blocks - 2:
            wait_halos(1, mid_halos)
        modes_ref[b * TILE : (b + 1) * TILE, :] = update(b, old(mid, 1, b - 1), old(mid, 1, b + 1))

    ids_now = ids_row.astype(jnp.int32)
    modes = modes_ref[...]
    group = IFACE // NEAR
    index = lax.broadcasted_iota(jnp.int32, (group, rows), 0)

    def share(target):
        chosen = jnp.where(index_target(target) == ids_now, values_row, 0.0)
        return dot(chosen, modes)

    def index_target(target):
        if not reduce_here:
            return index + target * group
        return (index // owned) * (NEAR * owned) + target * owned + lax.rem(index, owned)

    if not reduce_here:
        for k in range(NEAR):
            reduced_ref[k * group : (k + 1) * group, :] = share(k)
        return

    sent = []
    for k in range(1, NEAR):
        parts[k - 1] = share(lax.rem(lo + k, NEAR))
        copy = pltpu.make_async_remote_copy(
            src_ref=parts.at[k - 1],
            dst_ref=near_in.at[k - 1],
            send_sem=near_send.at[k - 1],
            recv_sem=near_recv.at[k - 1],
            device_id=near_ids[k - 1],
            device_id_type=MESH,
        )
        copy.start()
        sent.append(copy)
    total = share(lo)
    for k, copy in enumerate(sent):
        copy.wait()
        total = total + near_in[k]
    far_out[...] = total.reshape(far, owned, width)
    sent = []
    for k in range(1, far):
        copy = pltpu.make_async_remote_copy(
            src_ref=far_out.at[lax.rem(hi + k, far)],
            dst_ref=far_in.at[k - 1],
            send_sem=far_send.at[k - 1],
            recv_sem=far_recv.at[k - 1],
            device_id=far_ids[k - 1],
            device_id_type=MESH,
        )
        copy.start()
        sent.append(copy)
    result = boundary_ref[...] + far_out[hi]
    for k, copy in enumerate(sent):
        copy.wait()
        result = result + far_in[k]
    reduced_ref[...] = result


def on_device(
    diagonal_tiles,
    lower_tiles,
    upper_tiles,
    tile_pattern,
    interface_ids,
    coupling_values,
    warm_start,
    boundary_stiffness,
):
    slabs = lax.axis_size("slab")
    here = diagonal_tiles.shape[0]
    rows, width = warm_start.shape
    owned = boundary_stiffness.shape[0]
    reduce_here = slabs % NEAR == 0 and slabs > NEAR and owned % 8 == 0
    far = slabs // NEAR if reduce_here else 2
    inverses = tile_inverse(jnp.linalg.cholesky(diagonal_tiles))
    vmem = pl.BlockSpec(memory_space=pltpu.VMEM)
    f32 = jnp.float32
    sem = pltpu.SemaphoreType.DMA
    modes, reduced = pl.pallas_call(
        functools.partial(body, slabs, reduce_here),
        out_shape=(
            jax.ShapeDtypeStruct((rows, width), f32),
            jax.ShapeDtypeStruct((owned if reduce_here else IFACE, width), f32),
        ),
        in_specs=[pl.BlockSpec(memory_space=pltpu.SMEM)] + [vmem] * 7,
        out_specs=(vmem, vmem),
        scratch_shapes=[
            pltpu.VMEM((2 * here, TILE, 2 * TILE), f32),
            pltpu.VMEM((2 * here, TILE, TILE), f32),
            pltpu.VMEM((2 * SWEEPS, TILE, width), f32),
            pltpu.VMEM((rows, width), f32),
            pltpu.VMEM((NEAR - 1, IFACE // NEAR, width), f32),
            pltpu.VMEM((NEAR - 1, IFACE // NEAR, width), f32),
            pltpu.VMEM((far, owned, width), f32),
            pltpu.VMEM((far - 1, owned, width), f32),
            sem((2,)),
            sem((2,)),
            sem((2 * SWEEPS,)),
            sem((2 * SWEEPS,)),
            sem((NEAR - 1,)),
            sem((NEAR - 1,)),
            sem((far - 1,)),
            sem((far - 1,)),
        ],
        compiler_params=pltpu.CompilerParams(
            collective_id=0, has_side_effects=True, vmem_limit_bytes=40 * 1024 * 1024
        ),
    )(
        tile_pattern,
        inverses,
        lower_tiles,
        upper_tiles,
        interface_ids.reshape(1, rows),
        coupling_values.reshape(1, rows),
        warm_start,
        boundary_stiffness,
    )
    if not reduce_here:
        total = lax.psum(reduced, "slab")
        share = lax.dynamic_slice_in_dim(total, lax.axis_index("slab") * owned, owned)
        reduced = boundary_stiffness + share
    return (modes, reduced)


def solution(mesh):
    placed = (
        P(("slab", "col"), None, None),
        P(("slab", "col"), None, None),
        P(("slab", "col"), None, None),
        P(("slab", "col"), None),
        P("slab"),
        P("slab"),
        P("slab", "col"),
        P("slab", "col"),
    )
    return jax.shard_map(
        on_device,
        mesh=mesh,
        in_specs=placed,
        out_specs=(P("slab", "col"), P("slab", "col")),
        check_vma=False,
    )
```

time: 210 us -> 81.7 us (0.39)
  waiting for transfers between devices: 114 us -> 0 us
  Pallas kernels: 0 us -> 33.5 us
  blocking collectives: 14.6 us -> 0 us
  between operations: 14.3 us -> 0.78 us
  starting transfers between devices: 10.3 us -> 0 us
  matrix products: 6.22 us -> 0.65 us
    psum x1 -> x0, waiting for transfers between devices: 111 us -> none  [on_device(): lax.psum(jnp.dot(select, modes, precision=lax.Precision.HIGHEST, preferre...]
    pallas_call x0 -> x1, Pallas kernels: none -> 33.5 us  [on_device(): pl.pallas_call(functools.partial(body, slabs, reduce_here), out_shape=(ja...]
    all_to_all x2 -> x0, blocking collectives: 14.6 us -> none  [the longest x1 9.37 us: on_device(): lax.all_to_all(block_modes, 'col', split_axis=1, concat_axis=0, tiled=True)]
    ppermute x4 -> x0, starting transfers between devices: 10.3 us -> none  [the longest x2 7.51 us: extended_2(): before = lax.ppermute(last, axis, up)]
    dot_general x7 -> x0, matrix products: 5.57 us -> none  [the longest x1 1.84 us: on_device(): jnp.dot(select, modes, precision=lax.Precision.HIGHEST, preferred_element...]
    ppermute x4 -> x0, waiting for transfers between devices: 3.16 us -> none  [the longest x2 3.15 us: extended_2(): after = lax.ppermute(initial, axis, down)]
  transfers between devices with their start and end apart: 5 -> 0, of which waited for: 2 -> 0; matrix products, arithmetic and copies ran while one was open for 21% -> 0% of each run, Pallas kernels for 0% -> 0%
where the time goes in v1:
time: 81.7 us; the launch traced here: 81.5 us
  other arithmetic  43.4 us (53%)
  Pallas kernels  33.5 us (41%)
  local copies, waits for them, and re-layouts  3.13 us (4%)
    pallas_call x1, Pallas kernels, on_device(): pl.pallas_call(functools.partial(body, slabs, reduce_here), out_shape=(ja...  33.5 us
    another operation x4, other arithmetic, on_device(): inverses = tile_inverse(jnp.linalg.cholesky(diagonal_tiles))  23.6 us
    another operation x3, other arithmetic, tile_inverse(): lax.linalg.triangular_solve(factors, inner, left_side=True, lower=True, t...  19.8 us
    unnamed x19, local copies, waits for them, and re-layouts  3.13 us

profile of v1, /device:TPU:0, one launch (start us, length us, event | category | flops | bytes accessed | tf_op | source)
XLA Modules:
  0.0 81.5 jit_solution(16659868106699388967)
XLA Ops:
  0.7 0.0 copy-start.7
  0.7 1.1 %copy.11 = f32[2,128,128]{1,2,0:T(8,128)S(1)} copy(f32[2,128,128]{2,1,0:T(8,128)} %param.8) | data formatting | bytes 262144 | tf_op args[0]
  1.8 0.0 copy-done.7
  1.8 23.5 %custom-call.9 = f32[2,128,128]{2,1,0:T(8,128)S(1)} custom-call(f32[2,128,128]{2,1,0:T(8,128)S(1)} %fusion.4), custom_call_target="Cholesky" | custom-call | tf_op jit(solution)/shard_map/jit(cholesky)/cholesky | solution.py:264
  25.3 0.0 copy-start
  25.3 0.1 compare_reduce_fusion
  25.4 0.1 select_bitcast_fusion
  25.5 19.7 %custom-call.10 = f32[2,1,128,128]{2,3,1,0:T(8,128)S(1)} custom-call(f32[2,1,128,128]{3,2,1,0:T(8,128)S(1)} %select_bitcast_fusion), custom_call_target="InvertDiagBlocksLowerTriangular" | custom-call | tf_op jit(solution)/shard_map/triangular_solve | solution.py:23
  45.2 0.4 fusion.2
  45.6 0.0 copy-start.1
  45.6 0.0 copy-start.2
  45.6 0.0 copy-start.3
  45.6 0.0 copy-start.4
  45.6 0.0 copy-start.5
  45.7 0.0 copy-start.6
  45.7 0.3 fusion.inv_in
  45.9 0.0 copy-done
  46.0 0.6 copy-done.1
  46.5 0.1 copy-done.2
  46.6 0.0 copy-done.3
  46.6 0.0 copy-done.4
  46.6 0.0 copy-done.5
  46.6 0.0 copy-done.6
  46.6 33.5 %shard_map.95 = (f32[512,256]{1,0:T(8,128)S(1)}, f32[32,256]{1,0:T(8,128)S(1)}) custom-call(s32[2,2]{1,0:T(2,128)S(1)} %copy-done.6, f32[2,128,128]{2,1,0:T(8,128)S(1)} %fusion.inv_in, f32[2,128,128]{2,1,0:T(8,128)S(1)} %copy-done.1, f32[2,128,128]{2,1,0:T(8,128)S(1)} %copy-done.2, s32[1,512]{1,0:T(1,128)S(1)} %bitcast.14, f32[1,512]{1,0:T(1,128)S(1)} %bitcast.15, ...), custom_call_target="tpu_custom_call" | custom-call | tf_op jit(solution)/shard_map/pallas_call | solution.py:268
  80.1 0.8 copy.14
  80.9 0.6 copy.15
  (5 shorter events, 0.1 us)
Async XLA Ops:
  0.7 1.1 %copy-start.7 = (f32[2,128,128]{2,1,0:T(8,128)S(1)}, f32[2,128,128]{2,1,0:T(8,128)}, u32[]{:S(2)}) copy-start(f32[2,128,128]{2,1,0:T(8,128)} %param.8) | copy-start | bytes 393220
  25.3 20.6 %copy-start = (f32[512,256]{1,0:T(8,128)S(1)}, f32[512,256]{1,0:T(8,128)}, u32[]{:S(2)}) copy-start(f32[512,256]{1,0:T(8,128)} %warm_ref.1) | copy-start | bytes 1572868
  45.6 0.9 %copy-start.1 = (f32[2,128,128]{2,1,0:T(8,128)S(1)}, f32[2,128,128]{2,1,0:T(8,128)}, u32[]{:S(2)}) copy-start(f32[2,128,128]{2,1,0:T(8,128)} %lower_ref.1) | copy-start | bytes 393220
  45.6 1.0 %copy-start.2 = (f32[2,128,128]{2,1,0:T(8,128)S(1)}, f32[2,128,128]{2,1,0:T(8,128)}, u32[]{:S(2)}) copy-start(f32[2,128,128]{2,1,0:T(8,128)} %upper_ref.1) | copy-start | bytes 393220
  45.6 1.0 %copy-start.3 = (f32[32,256]{1,0:T(8,128)S(1)}, f32[32,256]{1,0:T(8,128)}, u32[]{:S(2)}) copy-start(f32[32,256]{1,0:T(8,128)} %boundary_ref.1) | copy-start | bytes 98308
  45.6 0.9 %copy-start.4 = (s32[512]{0:T(512)S(1)}, s32[512]{0:T(512)}, u32[]{:S(2)}) copy-start(s32[512]{0:T(512)} %param.12) | copy-start | bytes 6148
  45.6 0.9 %copy-start.5 = (f32[512]{0:T(512)S(1)}, f32[512]{0:T(512)}, u32[]{:S(2)}) copy-start(f32[512]{0:T(512)} %param.13) | copy-start | bytes 6148
  45.7 0.9 %copy-start.6 = (s32[2,2]{1,0:T(2,128)S(1)}, s32[2,2]{1,0:T(2,128)}, u32[]{:S(2)}) copy-start(s32[2,2]{1,0:T(2,128)} %pattern_ref.1) | copy-start | bytes 52

commit v2 on v1

--- a/solution.py
+++ b/solution.py
@@ -11,16 +11,58 @@
 TILE = 128
 SWEEPS = 2
 NEAR = 4
+SUB = 8
 HIGH = lax.Precision.HIGHEST
 MESH = pl.DeviceIdType.MESH
 
 
-def tile_inverse(factors):
-    count = factors.shape[0]
-    size = factors.shape[1]
-    identity = jnp.broadcast_to(jnp.eye(size, dtype=jnp.float32), (count, size, size))
-    inner = lax.linalg.triangular_solve(factors, identity, left_side=True, lower=True)
-    return lax.linalg.triangular_solve(factors, inner, left_side=True, lower=True, transpose_a=True)
+def swept(block):
+    size = len(block)
+    e = {(i, j): block[i][j] for i in range(size) for j in range(i, size)}
+    for k in range(size):
+        r = 1.0 / e[k, k]
+        c = [e[min(i, k), max(i, k)] for i in range(size)]
+        t = [x * r for x in c]
+        for i in range(size):
+            for j in range(i, size):
+                if i == k and j == k:
+                    e[i, j] = -r
+                elif i == k:
+                    e[i, j] = t[j]
+                elif j == k:
+                    e[i, j] = t[i]
+                else:
+                    e[i, j] = e[i, j] - c[i] * t[j]
+    return e
+
+
+def sweep_rows(ref, at, k):
+    first = pl.multiple_of(k * SUB, SUB)
+    panel = ref[at, pl.ds(first, SUB), :]
+    corner = pltpu.roll(panel, lax.rem(TILE - k * SUB, TILE), 1)
+    lanes = lax.broadcasted_iota(jnp.int32, (SUB, TILE), 1) - k * SUB
+    subs = lax.broadcasted_iota(jnp.int32, (SUB, TILE), 0)
+    wide = [jnp.broadcast_to(corner[:, j : j + 1], (SUB, TILE)) for j in range(SUB)]
+    table = [
+        [jnp.broadcast_to(wide[j][i : i + 1, :], (SUB, TILE)) if j >= i else None for j in range(SUB)]
+        for i in range(SUB)
+    ]
+    e = swept(table)
+    inside = (lanes >= 0) & (lanes < SUB)
+    source = jnp.where(inside, jnp.where(lanes == subs, 1.0, 0.0), -panel)
+    rows = None
+    for j in range(SUB):
+        column = e[0, j]
+        for i in range(1, SUB):
+            column = jnp.where(subs == i, e[min(i, j), max(i, j)], column)
+        term = column * jnp.broadcast_to(source[j : j + 1, :], (SUB, TILE))
+        rows = term if rows is None else rows + term
+    change = lax.dot_general(
+        panel, rows, (((0,), (0,)), ((), ())), precision=HIGH, preferred_element_type=jnp.float32
+    )
+    full = lax.broadcasted_iota(jnp.int32, (TILE, TILE), 1) - k * SUB
+    ref[at] = jnp.where((full >= 0) & (full < SUB), 0.0, ref[at]) - change
+    ref[at, pl.ds(first, SUB), :] = rows
 
 
 def dot(a, b):
@@ -31,7 +73,7 @@
     slabs,
     reduce_here,
     pattern_ref,
-    inv_in,
+    diagonal_ref,
     lower_ref,
     upper_ref,
     ids_ref,
@@ -79,7 +121,7 @@
         at = col * here + b
         lu[at, :, :TILE] = lower_ref[b] * pattern_ref[b, 0].astype(jnp.float32)
         lu[at, :, TILE:] = upper_ref[b] * pattern_ref[b, 1].astype(jnp.float32)
-        inv[at] = inv_in[b]
+        inv[at] = diagonal_ref[b]
 
     pl.semaphore_wait(barrier, len(partners))
 
@@ -149,9 +191,6 @@
     start_halos(warm_halos)
     tiles = pair(lu, 0)
     tiles.start()
-    inverses = pair(inv, 1)
-    inverses.start()
-
     rows = blocks * TILE
     ids_row = jnp.minimum(ids_ref[...], IFACE).astype(jnp.float32)
     values_row = values_ref[...]
@@ -163,12 +202,20 @@
         part = slice(b * TILE, (b + 1) * TILE)
         return jnp.where(ids_col[part] == columns, -values_col[part], 0.0)
 
+    def invert(k, carry):
+        for b in range(here):
+            sweep_rows(inv, col * here + b, k)
+        return carry
+
+    lax.fori_loop(0, TILE // SUB, invert, 0)
+    inverses = pair(inv, 1)
+    inverses.start()
     tiles.wait()
     inverses.wait()
 
     def update(b, below, above):
         both = jnp.concatenate([below, above], axis=0)
-        return dot(inv[b], right_side(b) - dot(lu[b], both))
+        return dot(inv[b], dot(lu[b], both) - right_side(b))
 
     def old(ref, step, b):
         if b < 0:
@@ -261,7 +308,6 @@
     owned = boundary_stiffness.shape[0]
     reduce_here = slabs % NEAR == 0 and slabs > NEAR and owned % 8 == 0
     far = slabs // NEAR if reduce_here else 2
-    inverses = tile_inverse(jnp.linalg.cholesky(diagonal_tiles))
     vmem = pl.BlockSpec(memory_space=pltpu.VMEM)
     f32 = jnp.float32
     sem = pltpu.SemaphoreType.DMA
@@ -296,7 +342,7 @@
         ),
     )(
         tile_pattern,
-        inverses,
+        diagonal_tiles,
         lower_tiles,
         upper_tiles,
         interface_ids.reshape(1, rows),

time: 81.7 us -> 54.9 us (0.67)
  other arithmetic: 43.4 us -> 0 us
  Pallas kernels: 33.5 us -> 46.6 us
  local copies, waits for them, and re-layouts: 3.13 us -> 7.28 us
    another operation x7 -> x0, other arithmetic: 43.4 us -> none  [the longest x4 23.6 us: on_device(): inverses = tile_inverse(jnp.linalg.cholesky(diagonal_tiles))]
    pallas_call x1, Pallas kernels: 33.5 us -> 46.6 us  [on_device(): pl.pallas_call(functools.partial(body, slabs, reduce_here), out_shape=(ja...]
    unnamed x19 -> x18, local copies, waits for them, and re-layouts: 3.13 us -> 7.28 us
where the time goes in v2:
time: 54.9 us; the launch traced here: 54.6 us
  Pallas kernels  46.6 us (85%)
  local copies, waits for them, and re-layouts  7.28 us (13%)
  between operations  0.66 us (1%)
    pallas_call x1, Pallas kernels, on_device(): pl.pallas_call(functools.partial(body, slabs, reduce_here), out_shape=(ja...  46.6 us
    unnamed x18, local copies, waits for them, and re-layouts  7.28 us

profile of v2, /device:TPU:0, one launch (start us, length us, event | category | flops | bytes accessed | tf_op | source)
XLA Modules:
  0.0 54.6 jit_solution(13392244139369039802)
XLA Ops:
  0.6 0.0 copy-start.5
  0.6 0.0 copy-start.7
  0.7 0.7 %copy-done.5 = s32[512]{0:T(512)S(1)} copy-done((s32[512]{0:T(512)S(1)}, s32[512]{0:T(512)}, u32[]{:S(2)}) %copy-start.5) | copy-done | bytes 2072
  1.3 0.0 copy-done.7
  1.3 0.0 copy-start
  1.3 1.0 %copy-done = f32[512,256]{1,0:T(8,128)S(1)} copy-done((f32[512,256]{1,0:T(8,128)S(1)}, f32[512,256]{1,0:T(8,128)}, u32[]{:S(2)}) %copy-start) | copy-done | bytes 524312
  2.4 0.0 copy-start.1
  2.4 0.9 %copy-done.1 = f32[2,128,128]{2,1,0:T(8,128)S(1)} copy-done((f32[2,128,128]{2,1,0:T(8,128)S(1)}, f32[2,128,128]{2,1,0:T(8,128)}, u32[]{:S(2)}) %copy-start.1) | copy-done | bytes 131096
  3.3 0.0 copy-start.2
  3.3 0.9 %copy-done.2 = f32[2,128,128]{2,1,0:T(8,128)S(1)} copy-done((f32[2,128,128]{2,1,0:T(8,128)S(1)}, f32[2,128,128]{2,1,0:T(8,128)}, u32[]{:S(2)}) %copy-start.2) | copy-done | bytes 131096
  4.2 0.0 copy-start.3
  4.2 0.9 %copy-done.3 = f32[2,128,128]{2,1,0:T(8,128)S(1)} copy-done((f32[2,128,128]{2,1,0:T(8,128)S(1)}, f32[2,128,128]{2,1,0:T(8,128)}, u32[]{:S(2)}) %copy-start.3) | copy-done | bytes 131096
  5.1 0.0 copy-start.4
  5.1 0.8 %copy-done.4 = f32[32,256]{1,0:T(8,128)S(1)} copy-done((f32[32,256]{1,0:T(8,128)S(1)}, f32[32,256]{1,0:T(8,128)}, u32[]{:S(2)}) %copy-start.4) | copy-done | bytes 32792
  5.8 0.0 copy-start.6
  5.8 0.7 %copy-done.6 = f32[512]{0:T(512)S(1)} copy-done((f32[512]{0:T(512)S(1)}, f32[512]{0:T(512)}, u32[]{:S(2)}) %copy-start.6) | copy-done | bytes 2072
  6.5 46.6 %shard_map.95 = (f32[512,256]{1,0:T(8,128)S(1)}, f32[32,256]{1,0:T(8,128)S(1)}) custom-call(s32[2,2]{1,0:T(2,128)S(1)} %copy-done.7, f32[2,128,128]{2,1,0:T(8,128)S(1)} %copy-done.1, f32[2,128,128]{2,1,0:T(8,128)S(1)} %copy-done.2, f32[2,128,128]{2,1,0:T(8,128)S(1)} %copy-done.3, s32[1,512]{1,0:T(1,128)S(1)} %bitcast.2, f32[1,512]{1,0:T(1,128)S(1)} %bitcast.3, ...), custom_call_target="tpu_custom_call" | custom-call | tf_op jit(solution)/shard_map/pallas_call | solution.py:314
  53.2 0.8 %copy.12 = f32[512,256]{1,0:T(8,128)} copy(f32[512,256]{1,0:T(8,128)S(1)} %get-tuple-element.4) | data formatting | bytes 1048576
  54.0 0.6 %copy.13 = f32[32,256]{1,0:T(8,128)} copy(f32[32,256]{1,0:T(8,128)S(1)} %get-tuple-element.5) | data formatting | bytes 65536
Async XLA Ops:
  0.6 0.7 %copy-start.5 = (s32[512]{0:T(512)S(1)}, s32[512]{0:T(512)}, u32[]{:S(2)}) copy-start(s32[512]{0:T(512)} %param.12) | copy-start | bytes 6148
  0.6 0.7 %copy-start.7 = (s32[2,2]{1,0:T(2,128)S(1)}, s32[2,2]{1,0:T(2,128)}, u32[]{:S(2)}) copy-start(s32[2,2]{1,0:T(2,128)} %pattern_ref.1) | copy-start | bytes 52
  1.3 1.0 %copy-start = (f32[512,256]{1,0:T(8,128)S(1)}, f32[512,256]{1,0:T(8,128)}, u32[]{:S(2)}) copy-start(f32[512,256]{1,0:T(8,128)} %warm_ref.1) | copy-start | bytes 1572868
  2.4 0.9 %copy-start.1 = (f32[2,128,128]{2,1,0:T(8,128)S(1)}, f32[2,128,128]{2,1,0:T(8,128)}, u32[]{:S(2)}) copy-start(f32[2,128,128]{2,1,0:T(8,128)} %diagonal_ref.1) | copy-start | bytes 393220
  3.3 0.9 %copy-start.2 = (f32[2,128,128]{2,1,0:T(8,128)S(1)}, f32[2,128,128]{2,1,0:T(8,128)}, u32[]{:S(2)}) copy-start(f32[2,128,128]{2,1,0:T(8,128)} %lower_ref.1) | copy-start | bytes 393220
  4.2 0.9 %copy-start.3 = (f32[2,128,128]{2,1,0:T(8,128)S(1)}, f32[2,128,128]{2,1,0:T(8,128)}, u32[]{:S(2)}) copy-start(f32[2,128,128]{2,1,0:T(8,128)} %upper_ref.1) | copy-start | bytes 393220
  5.1 0.8 %copy-start.4 = (f32[32,256]{1,0:T(8,128)S(1)}, f32[32,256]{1,0:T(8,128)}, u32[]{:S(2)}) copy-start(f32[32,256]{1,0:T(8,128)} %boundary_ref.1) | copy-start | bytes 98308
  5.8 0.7 %copy-start.6 = (f32[512]{0:T(512)S(1)}, f32[512]{0:T(512)}, u32[]{:S(2)}) copy-start(f32[512]{0:T(512)} %param.13) | copy-start | bytes 6148

commit v3 on v1

--- a/solution.py
+++ b/solution.py
@@ -11,27 +11,106 @@
 TILE = 128
 SWEEPS = 2
 NEAR = 4
-HIGH = lax.Precision.HIGHEST
+SUB = 8
 MESH = pl.DeviceIdType.MESH
 
 
-def tile_inverse(factors):
-    count = factors.shape[0]
-    size = factors.shape[1]
-    identity = jnp.broadcast_to(jnp.eye(size, dtype=jnp.float32), (count, size, size))
-    inner = lax.linalg.triangular_solve(factors, identity, left_side=True, lower=True)
-    return lax.linalg.triangular_solve(factors, inner, left_side=True, lower=True, transpose_a=True)
+def pieces(x, count):
+    out = []
+    for _ in range(count):
+        piece = x.astype(jnp.bfloat16).astype(jnp.float32)
+        out.append(piece)
+        x = x - piece
+    return out
+
+
+def swept(columns, subs):
+    tiles = range(len(columns))
+    for k in range(SUB):
+        pivots = [[jnp.broadcast_to(columns[t][k][j : j + 1, :], (SUB, TILE)) for j in range(SUB)] for t in tiles]
+        inverted = [1.0 / pivots[t][k] for t in tiles]
+        scaled = [columns[t][k] * inverted[t] for t in tiles]
+        here = subs == k
+        new = []
+        for t in tiles:
+            new.append(
+                [
+                    jnp.where(here, -inverted[t], scaled[t])
+                    if j == k
+                    else jnp.where(here, pivots[t][j] * inverted[t], columns[t][j] - scaled[t] * pivots[t][j])
+                    for j in range(SUB)
+                ]
+            )
+        columns = new
+    return columns
+
+
+def sweep_rows(ref, base, count, k):
+    first = pl.multiple_of(k * SUB, SUB)
+    tiles = range(count)
+    lanes = lax.broadcasted_iota(jnp.int32, (SUB, TILE), 1) - k * SUB
+    subs = lax.broadcasted_iota(jnp.int32, (SUB, TILE), 0)
+    inside = (lanes >= 0) & (lanes < SUB)
+    unit = jnp.where(lanes == subs, 1.0, 0.0)
+    full = lax.broadcasted_iota(jnp.int32, (TILE, TILE), 1) - k * SUB
+    outside = (full < 0) | (full >= SUB)
+    panels = [ref[base + t, pl.ds(first, SUB), :] for t in tiles]
+    shift = lax.rem(TILE - k * SUB, TILE)
+    corners = [pltpu.roll(panels[t], shift, 1) for t in tiles]
+    columns = [
+        [jnp.broadcast_to(corners[t][:, j : j + 1], (SUB, TILE)) for j in range(SUB)] for t in tiles
+    ]
+    left = []
+    for t in tiles:
+        a1, a2, a3 = pieces(panels[t], 3)
+        left.append(jnp.concatenate([a1, a1, a2, a1, a2, a3], axis=0).astype(jnp.bfloat16))
+    columns = swept(columns, subs)
+    rows = []
+    for t in tiles:
+        source = jnp.where(inside, unit, -panels[t])
+        terms = [columns[t][j] * jnp.broadcast_to(source[j : j + 1, :], (SUB, TILE)) for j in range(SUB)]
+        while len(terms) > 1:
+            terms = [terms[i] + terms[i + 1] for i in range(0, len(terms), 2)]
+        rows.append(terms[0])
+    changes = []
+    for t in tiles:
+        b1, b2, b3 = pieces(rows[t], 3)
+        right = jnp.concatenate([b1, b2, b1, b3, b2, b1], axis=0).astype(jnp.bfloat16)
+        changes.append(
+            lax.dot_general(left[t], right, (((0,), (0,)), ((), ())), preferred_element_type=jnp.float32)
+        )
+    for t in tiles:
+        ref[base + t] = jnp.where(outside, ref[base + t], 0.0) - changes[t]
+        ref[base + t, pl.ds(first, SUB), :] = rows[t]
+
+
+def split(x):
+    high = x.astype(jnp.bfloat16)
+    return high, (x - high.astype(jnp.float32)).astype(jnp.bfloat16)
+
+
+def product(a, b):
+    return jnp.dot(a, b, preferred_element_type=jnp.float32)
 
 
 def dot(a, b):
-    return jnp.dot(a, b, precision=HIGH, preferred_element_type=jnp.float32)
+    (ah, al), (bh, bl) = split(a), split(b)
+    return product(ah, bh) + (product(ah, bl) + product(al, bh))
 
 
 def body(
     slabs,
     reduce_here,
     pattern_ref,
-    inv_in,
+    diagonal_hbm,
+    lower_hbm,
+    upper_hbm,
+    ids_hbm,
+    values_hbm,
+    warm_hbm,
+    boundary_hbm,
+    modes_hbm,
+    reduced_hbm,
     lower_ref,
     upper_ref,
     ids_ref,
@@ -40,6 +119,7 @@
     boundary_ref,
     modes_ref,
     reduced_ref,
+    local,
     lu,
     inv,
     halo,
@@ -75,11 +155,21 @@
     for partner in partners:
         pl.semaphore_signal(barrier, inc=1, device_id=partner, device_id_type=MESH)
 
+    mine = pl.ds(col * here, here)
+    sources = [lower_hbm, upper_hbm, diagonal_hbm, warm_hbm, ids_hbm, values_hbm, boundary_hbm]
+    places = [lower_ref, upper_ref, inv.at[mine], warm_ref, ids_ref, values_ref, boundary_ref]
+    loads = [
+        pltpu.make_async_copy(source, place, local.at[i])
+        for i, (source, place) in enumerate(zip(sources, places))
+    ]
+    for load in loads:
+        load.start()
+    loads[0].wait()
+    loads[1].wait()
     for b in range(here):
         at = col * here + b
         lu[at, :, :TILE] = lower_ref[b] * pattern_ref[b, 0].astype(jnp.float32)
         lu[at, :, TILE:] = upper_ref[b] * pattern_ref[b, 1].astype(jnp.float32)
-        inv[at] = inv_in[b]
 
     pl.semaphore_wait(barrier, len(partners))
 
@@ -135,40 +225,45 @@
             halo[2 * step + 1] = jnp.zeros((TILE, width), jnp.float32)
 
     def pair(ref, which):
-        mine = ref.at[pl.ds(col * here, here)]
+        part = ref.at[mine]
         return pltpu.make_async_remote_copy(
-            src_ref=mine,
-            dst_ref=mine,
+            src_ref=part,
+            dst_ref=part,
             send_sem=pair_send.at[which],
             recv_sem=pair_recv.at[which],
             device_id=other,
             device_id_type=MESH,
         )
 
-    warm_halos = halos(0, warm_ref.at[pl.ds(0, TILE)], warm_ref.at[pl.ds((blocks - 1) * TILE, TILE)])
+    warm_halos = halos(0, warm_hbm.at[pl.ds(0, TILE)], warm_hbm.at[pl.ds((blocks - 1) * TILE, TILE)])
     start_halos(warm_halos)
     tiles = pair(lu, 0)
     tiles.start()
+    rows = blocks * TILE
+    loads[2].wait()
+
+    def invert(k, carry):
+        sweep_rows(inv, col * here, here, k)
+        return carry
+
+    lax.fori_loop(0, TILE // SUB, invert, 0)
     inverses = pair(inv, 1)
     inverses.start()
 
-    rows = blocks * TILE
+    for load in loads[3:]:
+        load.wait()
     ids_row = jnp.minimum(ids_ref[...], IFACE).astype(jnp.float32)
-    values_row = values_ref[...]
     ids_col = jnp.broadcast_to(ids_row, (8, rows)).T[:, :1].astype(jnp.int32)
-    values_col = jnp.broadcast_to(values_row, (8, rows)).T[:, :1]
+    values_col = jnp.broadcast_to(values_ref[...], (8, rows)).T[:, :1]
     columns = lax.broadcasted_iota(jnp.int32, (TILE, width), 1) + col * width
 
     def right_side(b):
         part = slice(b * TILE, (b + 1) * TILE)
         return jnp.where(ids_col[part] == columns, -values_col[part], 0.0)
 
-    tiles.wait()
-    inverses.wait()
-
-    def update(b, below, above):
+    def residual(b, below, above):
         both = jnp.concatenate([below, above], axis=0)
-        return dot(inv[b], right_side(b) - dot(lu[b], both))
+        return dot(lu[b], both) - right_side(b)
 
     def old(ref, step, b):
         if b < 0:
@@ -177,35 +272,50 @@
             return halo[2 * step + 1]
         return ref[b * TILE : (b + 1) * TILE, :]
 
+    tiles.wait()
     wait_halos(0, warm_halos)
     mid_halos = halos(1, mid.at[pl.ds(0, TILE)], mid.at[pl.ds((blocks - 1) * TILE, TILE)])
     order = [0, blocks - 1] + list(range(1, blocks - 1))
+    held = [residual(b, old(warm_ref, 0, b - 1), old(warm_ref, 0, b + 1)) for b in order]
+    inverses.wait()
     for n, b in enumerate(order):
-        mid[b * TILE : (b + 1) * TILE, :] = update(b, old(warm_ref, 0, b - 1), old(warm_ref, 0, b + 1))
+        mid[b * TILE : (b + 1) * TILE, :] = dot(inv[b], held[n])
         if n == 1:
             start_halos(mid_halos)
+    stores = []
     for n, b in enumerate(order[2:] + order[:2]):
         if n == blocks - 2:
             wait_halos(1, mid_halos)
-        modes_ref[b * TILE : (b + 1) * TILE, :] = update(b, old(mid, 1, b - 1), old(mid, 1, b + 1))
+        part = pl.ds(b * TILE, TILE)
+        modes_ref[part, :] = dot(inv[b], residual(b, old(mid, 1, b - 1), old(mid, 1, b + 1)))
+        store = pltpu.make_async_copy(modes_ref.at[part], modes_hbm.at[part], local.at[len(loads) + n])
+        store.start()
+        stores.append(store)
 
     ids_now = ids_row.astype(jnp.int32)
-    modes = modes_ref[...]
+    weighted_high, weighted_low = split(values_col * modes_ref[...])
     group = IFACE // NEAR
     index = lax.broadcasted_iota(jnp.int32, (group, rows), 0)
 
     def share(target):
-        chosen = jnp.where(index_target(target) == ids_now, values_row, 0.0)
-        return dot(chosen, modes)
+        chosen = jnp.where(index_target(target) == ids_now, 1.0, 0.0).astype(jnp.bfloat16)
+        return product(chosen, weighted_high) + product(chosen, weighted_low)
 
     def index_target(target):
         if not reduce_here:
             return index + target * group
         return (index // owned) * (NEAR * owned) + target * owned + lax.rem(index, owned)
 
+    def finish():
+        last = pltpu.make_async_copy(reduced_ref, reduced_hbm, local.at[len(loads) + blocks])
+        last.start()
+        for store in stores + [last]:
+            store.wait()
+
     if not reduce_here:
         for k in range(NEAR):
             reduced_ref[k * group : (k + 1) * group, :] = share(k)
+        finish()
         return
 
     sent = []
@@ -243,6 +353,7 @@
         copy.wait()
         result = result + far_in[k]
     reduced_ref[...] = result
+    finish()
 
 
 def on_device(
@@ -261,8 +372,7 @@
     owned = boundary_stiffness.shape[0]
     reduce_here = slabs % NEAR == 0 and slabs > NEAR and owned % 8 == 0
     far = slabs // NEAR if reduce_here else 2
-    inverses = tile_inverse(jnp.linalg.cholesky(diagonal_tiles))
-    vmem = pl.BlockSpec(memory_space=pltpu.VMEM)
+    hbm = pl.BlockSpec(memory_space=pl.ANY)
     f32 = jnp.float32
     sem = pltpu.SemaphoreType.DMA
     modes, reduced = pl.pallas_call(
@@ -271,9 +381,18 @@
             jax.ShapeDtypeStruct((rows, width), f32),
             jax.ShapeDtypeStruct((owned if reduce_here else IFACE, width), f32),
         ),
-        in_specs=[pl.BlockSpec(memory_space=pltpu.SMEM)] + [vmem] * 7,
-        out_specs=(vmem, vmem),
+        in_specs=[pl.BlockSpec(memory_space=pltpu.SMEM)] + [hbm] * 7,
+        out_specs=(hbm, hbm),
         scratch_shapes=[
+            pltpu.VMEM((here, TILE, TILE), f32),
+            pltpu.VMEM((here, TILE, TILE), f32),
+            pltpu.VMEM((1, rows), jnp.int32),
+            pltpu.VMEM((1, rows), f32),
+            pltpu.VMEM((rows, width), f32),
+            pltpu.VMEM((owned, width), f32),
+            pltpu.VMEM((rows, width), f32),
+            pltpu.VMEM((owned if reduce_here else IFACE, width), f32),
+            sem((8 + 2 * here,)),
             pltpu.VMEM((2 * here, TILE, 2 * TILE), f32),
             pltpu.VMEM((2 * here, TILE, TILE), f32),
             pltpu.VMEM((2 * SWEEPS, TILE, width), f32),
@@ -296,7 +415,7 @@
         ),
     )(
         tile_pattern,
-        inverses,
+        diagonal_tiles,
         lower_tiles,
         upper_tiles,
         interface_ids.reshape(1, rows),

time: 81.7 us -> 43.6 us (0.53)
  other arithmetic: 43.4 us -> 0 us
  local copies, waits for them, and re-layouts: 3.13 us -> 7.28 us
  Pallas kernels: 33.5 us -> 35.3 us
    another operation x7 -> x0, other arithmetic: 43.4 us -> none  [the longest x4 23.6 us: on_device(): inverses = tile_inverse(jnp.linalg.cholesky(diagonal_tiles))]
    unnamed x19 -> x18, local copies, waits for them, and re-layouts: 3.13 us -> 7.28 us
    pallas_call x1, Pallas kernels: 33.5 us -> 35.3 us  [on_device(): pl.pallas_call(functools.partial(body, slabs, reduce_here), out_shape=(ja...]
where the time goes in v3:
time: 43.6 us; the launch traced here: 43.3 us
  Pallas kernels  35.3 us (81%)
  local copies, waits for them, and re-layouts  7.28 us (17%)
  between operations  0.66 us (2%)
    pallas_call x1, Pallas kernels, on_device(): pl.pallas_call(functools.partial(body, slabs, reduce_here), out_shape=(ja...  35.3 us
    unnamed x18, local copies, waits for them, and re-layouts  7.28 us

profile of v3, /device:TPU:0, one launch (start us, length us, event | category | flops | bytes accessed | tf_op | source)
XLA Modules:
  0.0 43.3 jit_solution(18365725547578458452)
XLA Ops:
  0.6 0.0 copy-start.5
  0.6 0.0 copy-start.7
  0.7 0.7 %copy-done.5 = s32[512]{0:T(512)S(1)} copy-done((s32[512]{0:T(512)S(1)}, s32[512]{0:T(512)}, u32[]{:S(2)}) %copy-start.5) | copy-done | bytes 2072
  1.3 0.0 copy-done.7
  1.3 0.0 copy-start
  1.3 1.0 %copy-done = f32[512,256]{1,0:T(8,128)S(1)} copy-done((f32[512,256]{1,0:T(8,128)S(1)}, f32[512,256]{1,0:T(8,128)}, u32[]{:S(2)}) %copy-start) | copy-done | bytes 524312
  2.4 0.0 copy-start.1
  2.4 0.9 %copy-done.1 = f32[2,128,128]{2,1,0:T(8,128)S(1)} copy-done((f32[2,128,128]{2,1,0:T(8,128)S(1)}, f32[2,128,128]{2,1,0:T(8,128)}, u32[]{:S(2)}) %copy-start.1) | copy-done | bytes 131096
  3.3 0.0 copy-start.2
  3.3 0.9 %copy-done.2 = f32[2,128,128]{2,1,0:T(8,128)S(1)} copy-done((f32[2,128,128]{2,1,0:T(8,128)S(1)}, f32[2,128,128]{2,1,0:T(8,128)}, u32[]{:S(2)}) %copy-start.2) | copy-done | bytes 131096
  4.2 0.0 copy-start.3
  4.2 0.9 %copy-done.3 = f32[2,128,128]{2,1,0:T(8,128)S(1)} copy-done((f32[2,128,128]{2,1,0:T(8,128)S(1)}, f32[2,128,128]{2,1,0:T(8,128)}, u32[]{:S(2)}) %copy-start.3) | copy-done | bytes 131096
  5.1 0.0 copy-start.4
  5.1 0.8 %copy-done.4 = f32[32,256]{1,0:T(8,128)S(1)} copy-done((f32[32,256]{1,0:T(8,128)S(1)}, f32[32,256]{1,0:T(8,128)}, u32[]{:S(2)}) %copy-start.4) | copy-done | bytes 32792
  5.8 0.0 copy-start.6
  5.8 0.7 %copy-done.6 = f32[512]{0:T(512)S(1)} copy-done((f32[512]{0:T(512)S(1)}, f32[512]{0:T(512)}, u32[]{:S(2)}) %copy-start.6) | copy-done | bytes 2072
  6.5 35.3 %shard_map.95 = (f32[512,256]{1,0:T(8,128)S(1)}, f32[32,256]{1,0:T(8,128)S(1)}) custom-call(s32[2,2]{1,0:T(2,128)S(1)} %copy-done.7, f32[2,128,128]{2,1,0:T(8,128)S(1)} %copy-done.1, f32[2,128,128]{2,1,0:T(8,128)S(1)} %copy-done.2, f32[2,128,128]{2,1,0:T(8,128)S(1)} %copy-done.3, s32[1,512]{1,0:T(1,128)S(1)} %bitcast.2, f32[1,512]{1,0:T(1,128)S(1)} %bitcast.3, ...), custom_call_target="tpu_custom_call" | custom-call | tf_op jit(solution)/shard_map/pallas_call | solution.py:378
  41.9 0.8 %copy.12 = f32[512,256]{1,0:T(8,128)} copy(f32[512,256]{1,0:T(8,128)S(1)} %get-tuple-element.4) | data formatting | bytes 1048576
  42.7 0.6 %copy.13 = f32[32,256]{1,0:T(8,128)} copy(f32[32,256]{1,0:T(8,128)S(1)} %get-tuple-element.5) | data formatting | bytes 65536
Async XLA Ops:
  0.6 0.7 %copy-start.5 = (s32[512]{0:T(512)S(1)}, s32[512]{0:T(512)}, u32[]{:S(2)}) copy-start(s32[512]{0:T(512)} %param.12) | copy-start | bytes 6148
  0.6 0.7 %copy-start.7 = (s32[2,2]{1,0:T(2,128)S(1)}, s32[2,2]{1,0:T(2,128)}, u32[]{:S(2)}) copy-start(s32[2,2]{1,0:T(2,128)} %pattern_ref.1) | copy-start | bytes 52
  1.3 1.0 %copy-start = (f32[512,256]{1,0:T(8,128)S(1)}, f32[512,256]{1,0:T(8,128)}, u32[]{:S(2)}) copy-start(f32[512,256]{1,0:T(8,128)} %warm_hbm.1) | copy-start | bytes 1572868
  2.4 0.9 %copy-start.1 = (f32[2,128,128]{2,1,0:T(8,128)S(1)}, f32[2,128,128]{2,1,0:T(8,128)}, u32[]{:S(2)}) copy-start(f32[2,128,128]{2,1,0:T(8,128)} %diagonal_hbm.1) | copy-start | bytes 393220
  3.3 0.9 %copy-start.2 = (f32[2,128,128]{2,1,0:T(8,128)S(1)}, f32[2,128,128]{2,1,0:T(8,128)}, u32[]{:S(2)}) copy-start(f32[2,128,128]{2,1,0:T(8,128)} %lower_hbm.1) | copy-start | bytes 393220
  4.2 0.9 %copy-start.3 = (f32[2,128,128]{2,1,0:T(8,128)S(1)}, f32[2,128,128]{2,1,0:T(8,128)}, u32[]{:S(2)}) copy-start(f32[2,128,128]{2,1,0:T(8,128)} %upper_hbm.1) | copy-start | bytes 393220
  5.1 0.8 %copy-start.4 = (f32[32,256]{1,0:T(8,128)S(1)}, f32[32,256]{1,0:T(8,128)}, u32[]{:S(2)}) copy-start(f32[32,256]{1,0:T(8,128)} %boundary_hbm.1) | copy-start | bytes 98308
  5.8 0.7 %copy-start.6 = (f32[512]{0:T(512)S(1)}, f32[512]{0:T(512)}, u32[]{:S(2)}) copy-start(f32[512]{0:T(512)} %param.13) | copy-start | bytes 6148

commit v4 on v3

--- a/solution.py
+++ b/solution.py
@@ -156,22 +156,20 @@
         pl.semaphore_signal(barrier, inc=1, device_id=partner, device_id_type=MESH)
 
     mine = pl.ds(col * here, here)
-    sources = [lower_hbm, upper_hbm, diagonal_hbm, warm_hbm, ids_hbm, values_hbm, boundary_hbm]
-    places = [lower_ref, upper_ref, inv.at[mine], warm_ref, ids_ref, values_ref, boundary_ref]
+    sources = [diagonal_hbm, lower_hbm, upper_hbm, warm_hbm, ids_hbm, values_hbm, boundary_hbm]
+    places = [inv.at[mine], lower_ref, upper_ref, warm_ref, ids_ref, values_ref, boundary_ref]
     loads = [
         pltpu.make_async_copy(source, place, local.at[i])
         for i, (source, place) in enumerate(zip(sources, places))
     ]
     for load in loads:
         load.start()
-    loads[0].wait()
     loads[1].wait()
+    loads[2].wait()
     for b in range(here):
         at = col * here + b
         lu[at, :, :TILE] = lower_ref[b] * pattern_ref[b, 0].astype(jnp.float32)
         lu[at, :, TILE:] = upper_ref[b] * pattern_ref[b, 1].astype(jnp.float32)
-
-    pl.semaphore_wait(barrier, len(partners))
 
     def halos(step, first_block, last_block):
         down = pltpu.make_async_remote_copy(
@@ -236,17 +234,20 @@
         )
 
     warm_halos = halos(0, warm_hbm.at[pl.ds(0, TILE)], warm_hbm.at[pl.ds((blocks - 1) * TILE, TILE)])
-    start_halos(warm_halos)
     tiles = pair(lu, 0)
-    tiles.start()
     rows = blocks * TILE
-    loads[2].wait()
+    loads[0].wait()
 
     def invert(k, carry):
         sweep_rows(inv, col * here, here, k)
         return carry
 
-    lax.fori_loop(0, TILE // SUB, invert, 0)
+    early = TILE // SUB // 4
+    lax.fori_loop(0, early, invert, 0)
+    pl.semaphore_wait(barrier, len(partners))
+    start_halos(warm_halos)
+    tiles.start()
+    lax.fori_loop(early, TILE // SUB, invert, 0)
     inverses = pair(inv, 1)
     inverses.start()
 
@@ -297,9 +298,11 @@
     group = IFACE // NEAR
     index = lax.broadcasted_iota(jnp.int32, (group, rows), 0)
 
-    def share(target):
-        chosen = jnp.where(index_target(target) == ids_now, 1.0, 0.0).astype(jnp.bfloat16)
-        return product(chosen, weighted_high) + product(chosen, weighted_low)
+    def pick(target):
+        return jnp.where(index_target(target) == ids_now, 1.0, 0.0).astype(jnp.bfloat16)
+
+    def share(chosen, part=slice(None)):
+        return product(chosen, weighted_high[:, part]) + product(chosen, weighted_low[:, part])
 
     def index_target(target):
         if not reduce_here:
@@ -314,45 +317,52 @@
 
     if not reduce_here:
         for k in range(NEAR):
-            reduced_ref[k * group : (k + 1) * group, :] = share(k)
+            reduced_ref[k * group : (k + 1) * group, :] = share(pick(k))
         finish()
         return
 
-    sent = []
-    for k in range(1, NEAR):
-        parts[k - 1] = share(lax.rem(lo + k, NEAR))
-        copy = pltpu.make_async_remote_copy(
-            src_ref=parts.at[k - 1],
-            dst_ref=near_in.at[k - 1],
-            send_sem=near_send.at[k - 1],
-            recv_sem=near_recv.at[k - 1],
-            device_id=near_ids[k - 1],
-            device_id_type=MESH,
-        )
-        copy.start()
-        sent.append(copy)
-    total = share(lo)
-    for k, copy in enumerate(sent):
-        copy.wait()
-        total = total + near_in[k]
-    far_out[...] = total.reshape(far, owned, width)
-    sent = []
-    for k in range(1, far):
-        copy = pltpu.make_async_remote_copy(
-            src_ref=far_out.at[lax.rem(hi + k, far)],
-            dst_ref=far_in.at[k - 1],
-            send_sem=far_send.at[k - 1],
-            recv_sem=far_recv.at[k - 1],
-            device_id=far_ids[k - 1],
-            device_id_type=MESH,
-        )
-        copy.start()
-        sent.append(copy)
-    result = boundary_ref[...] + far_out[hi]
-    for k, copy in enumerate(sent):
-        copy.wait()
-        result = result + far_in[k]
-    reduced_ref[...] = result
+    half = width // 2
+    halves = [slice(0, half), slice(half, width)]
+    chosen = [pick(lax.rem(lo + k, NEAR)) for k in range(NEAR)]
+    near_sent = []
+    for h, part in enumerate(halves):
+        for k in range(1, NEAR):
+            parts[h, k - 1] = share(chosen[k], part)
+            copy = pltpu.make_async_remote_copy(
+                src_ref=parts.at[h, k - 1],
+                dst_ref=near_in.at[h, k - 1],
+                send_sem=near_send.at[h, k - 1],
+                recv_sem=near_recv.at[h, k - 1],
+                device_id=near_ids[k - 1],
+                device_id_type=MESH,
+            )
+            copy.start()
+            near_sent.append(copy)
+    totals = [share(chosen[0], part) for part in halves]
+    far_sent = []
+    for h in range(2):
+        total = totals[h]
+        for k in range(NEAR - 1):
+            near_sent[h * (NEAR - 1) + k].wait()
+            total = total + near_in[h, k]
+        far_out[h] = total.reshape(far, owned, half)
+        for k in range(1, far):
+            copy = pltpu.make_async_remote_copy(
+                src_ref=far_out.at[h, lax.rem(hi + k, far)],
+                dst_ref=far_in.at[h, k - 1],
+                send_sem=far_send.at[h, k - 1],
+                recv_sem=far_recv.at[h, k - 1],
+                device_id=far_ids[k - 1],
+                device_id_type=MESH,
+            )
+            copy.start()
+            far_sent.append(copy)
+    for h, part in enumerate(halves):
+        result = boundary_ref[:, part] + far_out[h, hi]
+        for k in range(far - 1):
+            far_sent[h * (far - 1) + k].wait()
+            result = result + far_in[h, k]
+        reduced_ref[:, part] = result
     finish()
 
 
@@ -372,7 +382,7 @@
     owned = boundary_stiffness.shape[0]
     reduce_here = slabs % NEAR == 0 and slabs > NEAR and owned % 8 == 0
     far = slabs // NEAR if reduce_here else 2
-    hbm = pl.BlockSpec(memory_space=pl.ANY)
+    hbm = pl.BlockSpec(memory_space=pltpu.HBM)
     f32 = jnp.float32
     sem = pltpu.SemaphoreType.DMA
     modes, reduced = pl.pallas_call(
@@ -397,18 +407,18 @@
             pltpu.VMEM((2 * here, TILE, TILE), f32),
             pltpu.VMEM((2 * SWEEPS, TILE, width), f32),
             pltpu.VMEM((rows, width), f32),
-            pltpu.VMEM((NEAR - 1, IFACE // NEAR, width), f32),
-            pltpu.VMEM((NEAR - 1, IFACE // NEAR, width), f32),
-            pltpu.VMEM((far, owned, width), f32),
-            pltpu.VMEM((far - 1, owned, width), f32),
+            pltpu.VMEM((2, NEAR - 1, IFACE // NEAR, width // 2), f32),
+            pltpu.VMEM((2, NEAR - 1, IFACE // NEAR, width // 2), f32),
+            pltpu.VMEM((2, far, owned, width // 2), f32),
+            pltpu.VMEM((2, far - 1, owned, width // 2), f32),
             sem((2,)),
             sem((2,)),
             sem((2 * SWEEPS,)),
             sem((2 * SWEEPS,)),
-            sem((NEAR - 1,)),
-            sem((NEAR - 1,)),
-            sem((far - 1,)),
-            sem((far - 1,)),
+            sem((2, NEAR - 1)),
+            sem((2, NEAR - 1)),
+            sem((2, far - 1)),
+            sem((2, far - 1)),
         ],
         compiler_params=pltpu.CompilerParams(
             collective_id=0, has_side_effects=True, vmem_limit_bytes=40 * 1024 * 1024

time: 43.6 us -> 43.3 us (level)
  no operation moved by 1% of the time
where the time goes in v4:
time: 43.3 us; the launch traced here: 43 us
  Pallas kernels  35 us (81%)
  local copies, waits for them, and re-layouts  7.28 us (17%)
  between operations  0.66 us (2%)
    pallas_call x1, Pallas kernels, on_device(): pl.pallas_call(functools.partial(body, slabs, reduce_here), out_shape=(ja...  35 us
    unnamed x18, local copies, waits for them, and re-layouts  7.28 us

profile of v4, /device:TPU:0, one launch (start us, length us, event | category | flops | bytes accessed | tf_op | source)
XLA Modules:
  0.0 43.0 jit_solution(10571729268558691396)
XLA Ops:
  0.6 0.0 copy-start.5
  0.6 0.0 copy-start.7
  0.7 0.7 %copy-done.5 = s32[512]{0:T(512)S(1)} copy-done((s32[512]{0:T(512)S(1)}, s32[512]{0:T(512)}, u32[]{:S(2)}) %copy-start.5) | copy-done | bytes 2072
  1.3 0.0 copy-done.7
  1.3 0.0 copy-start
  1.3 1.0 %copy-done = f32[512,256]{1,0:T(8,128)S(1)} copy-done((f32[512,256]{1,0:T(8,128)S(1)}, f32[512,256]{1,0:T(8,128)}, u32[]{:S(2)}) %copy-start) | copy-done | bytes 524312
  2.4 0.0 copy-start.1
  2.4 0.9 %copy-done.1 = f32[2,128,128]{2,1,0:T(8,128)S(1)} copy-done((f32[2,128,128]{2,1,0:T(8,128)S(1)}, f32[2,128,128]{2,1,0:T(8,128)}, u32[]{:S(2)}) %copy-start.1) | copy-done | bytes 131096
  3.3 0.0 copy-start.2
  3.3 0.9 %copy-done.2 = f32[2,128,128]{2,1,0:T(8,128)S(1)} copy-done((f32[2,128,128]{2,1,0:T(8,128)S(1)}, f32[2,128,128]{2,1,0:T(8,128)}, u32[]{:S(2)}) %copy-start.2) | copy-done | bytes 131096
  4.2 0.0 copy-start.3
  4.2 0.9 %copy-done.3 = f32[2,128,128]{2,1,0:T(8,128)S(1)} copy-done((f32[2,128,128]{2,1,0:T(8,128)S(1)}, f32[2,128,128]{2,1,0:T(8,128)}, u32[]{:S(2)}) %copy-start.3) | copy-done | bytes 131096
  5.1 0.0 copy-start.4
  5.1 0.8 %copy-done.4 = f32[32,256]{1,0:T(8,128)S(1)} copy-done((f32[32,256]{1,0:T(8,128)S(1)}, f32[32,256]{1,0:T(8,128)}, u32[]{:S(2)}) %copy-start.4) | copy-done | bytes 32792
  5.8 0.0 copy-start.6
  5.8 0.7 %copy-done.6 = f32[512]{0:T(512)S(1)} copy-done((f32[512]{0:T(512)S(1)}, f32[512]{0:T(512)}, u32[]{:S(2)}) %copy-start.6) | copy-done | bytes 2072
  6.5 35.0 %shard_map.95 = (f32[512,256]{1,0:T(8,128)S(1)}, f32[32,256]{1,0:T(8,128)S(1)}) custom-call(s32[2,2]{1,0:T(2,128)S(1)} %copy-done.7, f32[2,128,128]{2,1,0:T(8,128)S(1)} %copy-done.1, f32[2,128,128]{2,1,0:T(8,128)S(1)} %copy-done.2, f32[2,128,128]{2,1,0:T(8,128)S(1)} %copy-done.3, s32[1,512]{1,0:T(1,128)S(1)} %bitcast.2, f32[1,512]{1,0:T(1,128)S(1)} %bitcast.3, ...), custom_call_target="tpu_custom_call" | custom-call | tf_op jit(solution)/shard_map/pallas_call | solution.py:388
  41.5 0.8 %copy.12 = f32[512,256]{1,0:T(8,128)} copy(f32[512,256]{1,0:T(8,128)S(1)} %get-tuple-element.4) | data formatting | bytes 1048576
  42.3 0.6 %copy.13 = f32[32,256]{1,0:T(8,128)} copy(f32[32,256]{1,0:T(8,128)S(1)} %get-tuple-element.5) | data formatting | bytes 65536
Async XLA Ops:
  0.6 0.7 %copy-start.5 = (s32[512]{0:T(512)S(1)}, s32[512]{0:T(512)}, u32[]{:S(2)}) copy-start(s32[512]{0:T(512)} %param.12) | copy-start | bytes 6148
  0.6 0.7 %copy-start.7 = (s32[2,2]{1,0:T(2,128)S(1)}, s32[2,2]{1,0:T(2,128)}, u32[]{:S(2)}) copy-start(s32[2,2]{1,0:T(2,128)} %pattern_ref.1) | copy-start | bytes 52
  1.3 1.0 %copy-start = (f32[512,256]{1,0:T(8,128)S(1)}, f32[512,256]{1,0:T(8,128)}, u32[]{:S(2)}) copy-start(f32[512,256]{1,0:T(8,128)} %warm_hbm.1) | copy-start | bytes 1572868
  2.4 0.9 %copy-start.1 = (f32[2,128,128]{2,1,0:T(8,128)S(1)}, f32[2,128,128]{2,1,0:T(8,128)}, u32[]{:S(2)}) copy-start(f32[2,128,128]{2,1,0:T(8,128)} %diagonal_hbm.1) | copy-start | bytes 393220
  3.3 0.9 %copy-start.2 = (f32[2,128,128]{2,1,0:T(8,128)S(1)}, f32[2,128,128]{2,1,0:T(8,128)}, u32[]{:S(2)}) copy-start(f32[2,128,128]{2,1,0:T(8,128)} %lower_hbm.1) | copy-start | bytes 393220
  4.2 0.9 %copy-start.3 = (f32[2,128,128]{2,1,0:T(8,128)S(1)}, f32[2,128,128]{2,1,0:T(8,128)}, u32[]{:S(2)}) copy-start(f32[2,128,128]{2,1,0:T(8,128)} %upper_hbm.1) | copy-start | bytes 393220
  5.1 0.8 %copy-start.4 = (f32[32,256]{1,0:T(8,128)S(1)}, f32[32,256]{1,0:T(8,128)}, u32[]{:S(2)}) copy-start(f32[32,256]{1,0:T(8,128)} %boundary_hbm.1) | copy-start | bytes 98308
  5.8 0.7 %copy-start.6 = (f32[512]{0:T(512)S(1)}, f32[512]{0:T(512)}, u32[]{:S(2)}) copy-start(f32[512]{0:T(512)} %param.13) | copy-start | bytes 6148

commit v5 on v4

--- a/solution.py
+++ b/solution.py
@@ -109,16 +109,14 @@
     values_hbm,
     warm_hbm,
     boundary_hbm,
-    modes_hbm,
-    reduced_hbm,
+    modes_ref,
+    reduced_ref,
     lower_ref,
     upper_ref,
     ids_ref,
     values_ref,
     warm_ref,
     boundary_ref,
-    modes_ref,
-    reduced_ref,
     local,
     lu,
     inv,
@@ -283,15 +281,11 @@
         mid[b * TILE : (b + 1) * TILE, :] = dot(inv[b], held[n])
         if n == 1:
             start_halos(mid_halos)
-    stores = []
     for n, b in enumerate(order[2:] + order[:2]):
         if n == blocks - 2:
             wait_halos(1, mid_halos)
         part = pl.ds(b * TILE, TILE)
         modes_ref[part, :] = dot(inv[b], residual(b, old(mid, 1, b - 1), old(mid, 1, b + 1)))
-        store = pltpu.make_async_copy(modes_ref.at[part], modes_hbm.at[part], local.at[len(loads) + n])
-        store.start()
-        stores.append(store)
 
     ids_now = ids_row.astype(jnp.int32)
     weighted_high, weighted_low = split(values_col * modes_ref[...])
@@ -309,16 +303,9 @@
             return index + target * group
         return (index // owned) * (NEAR * owned) + target * owned + lax.rem(index, owned)
 
-    def finish():
-        last = pltpu.make_async_copy(reduced_ref, reduced_hbm, local.at[len(loads) + blocks])
-        last.start()
-        for store in stores + [last]:
-            store.wait()
-
     if not reduce_here:
         for k in range(NEAR):
             reduced_ref[k * group : (k + 1) * group, :] = share(pick(k))
-        finish()
         return
 
     half = width // 2
@@ -363,7 +350,6 @@
             far_sent[h * (far - 1) + k].wait()
             result = result + far_in[h, k]
         reduced_ref[:, part] = result
-    finish()
 
 
 def on_device(
@@ -392,7 +378,7 @@
             jax.ShapeDtypeStruct((owned if reduce_here else IFACE, width), f32),
         ),
         in_specs=[pl.BlockSpec(memory_space=pltpu.SMEM)] + [hbm] * 7,
-        out_specs=(hbm, hbm),
+        out_specs=(pl.BlockSpec(memory_space=pltpu.VMEM),) * 2,
         scratch_shapes=[
             pltpu.VMEM((here, TILE, TILE), f32),
             pltpu.VMEM((here, TILE, TILE), f32),
@@ -400,9 +386,7 @@
             pltpu.VMEM((1, rows), f32),
             pltpu.VMEM((rows, width), f32),
             pltpu.VMEM((owned, width), f32),
-            pltpu.VMEM((rows, width), f32),
-            pltpu.VMEM((owned if reduce_here else IFACE, width), f32),
-            sem((8 + 2 * here,)),
+            sem((7,)),
             pltpu.VMEM((2 * here, TILE, 2 * TILE), f32),
             pltpu.VMEM((2 * here, TILE, TILE), f32),
             pltpu.VMEM((2 * SWEEPS, TILE, width), f32),
@@ -424,14 +408,19 @@
             collective_id=0, has_side_effects=True, vmem_limit_bytes=40 * 1024 * 1024
         ),
     )(
-        tile_pattern,
-        diagonal_tiles,
-        lower_tiles,
-        upper_tiles,
-        interface_ids.reshape(1, rows),
-        coupling_values.reshape(1, rows),
-        warm_start,
-        boundary_stiffness,
+        *(
+            pltpu.with_memory_space_constraint(x, pltpu.HBM)
+            for x in (
+                tile_pattern,
+                diagonal_tiles,
+                lower_tiles,
+                upper_tiles,
+                interface_ids.reshape(1, rows),
+                coupling_values.reshape(1, rows),
+                warm_start,
+                boundary_stiffness,
+            )
+        ),
     )
     if not reduce_here:
         total = lax.psum(reduced, "slab")

time: 43.3 us -> 36.9 us (0.85)
  local copies, waits for them, and re-layouts: 7.28 us -> 1.41 us
    unnamed x18 -> x2, local copies, waits for them, and re-layouts: 7.28 us -> 1.41 us
where the time goes in v5:
time: 36.9 us; the launch traced here: 36.8 us
  Pallas kernels  34.7 us (94%)
  local copies, waits for them, and re-layouts  1.41 us (4%)
  between operations  0.64 us (2%)
    pallas_call x1, Pallas kernels, on_device(): pl.pallas_call(functools.partial(body, slabs, reduce_here), out_shape=(ja...  34.7 us
    unnamed x2, local copies, waits for them, and re-layouts  1.41 us

profile of v5, /device:TPU:0, one launch (start us, length us, event | category | flops | bytes accessed | tf_op | source)
XLA Modules:
  0.0 36.8 jit_solution(1864207389612756136)
XLA Ops:
  0.6 34.7 %shard_map.95 = (f32[512,256]{1,0:T(8,128)S(1)}, f32[32,256]{1,0:T(8,128)S(1)}) custom-call(s32[2,2]{1,0:T(2,128)} %pattern_ref.1, f32[2,128,128]{2,1,0:T(8,128)} %diagonal_hbm.1, f32[2,128,128]{2,1,0:T(8,128)} %lower_hbm.1, f32[2,128,128]{2,1,0:T(8,128)} %upper_hbm.1, s32[1,512]{1,0:T(1,128)} %bitcast.2, f32[1,512]{1,0:T(1,128)} %bitcast.3, ...), custom_call_target="tpu_custom_call" | custom-call | tf_op jit(solution)/shard_map/pallas_call | solution.py:374
  35.3 0.8 %copy.12 = f32[512,256]{1,0:T(8,128)} copy(f32[512,256]{1,0:T(8,128)S(1)} %get-tuple-element.4) | data formatting | bytes 1048576
  36.1 0.6 %copy.13 = f32[32,256]{1,0:T(8,128)} copy(f32[32,256]{1,0:T(8,128)S(1)} %get-tuple-element.5) | data formatting | bytes 65536

commit v6 on v5

--- a/solution.py
+++ b/solution.py
@@ -162,13 +162,6 @@
     ]
     for load in loads:
         load.start()
-    loads[1].wait()
-    loads[2].wait()
-    for b in range(here):
-        at = col * here + b
-        lu[at, :, :TILE] = lower_ref[b] * pattern_ref[b, 0].astype(jnp.float32)
-        lu[at, :, TILE:] = upper_ref[b] * pattern_ref[b, 1].astype(jnp.float32)
-
     def halos(step, first_block, last_block):
         down = pltpu.make_async_remote_copy(
             src_ref=first_block,
@@ -242,6 +235,12 @@
 
     early = TILE // SUB // 4
     lax.fori_loop(0, early, invert, 0)
+    loads[1].wait()
+    loads[2].wait()
+    for b in range(here):
+        at = col * here + b
+        lu[at, :, :TILE] = lower_ref[b] * pattern_ref[b, 0].astype(jnp.float32)
+        lu[at, :, TILE:] = upper_ref[b] * pattern_ref[b, 1].astype(jnp.float32)
     pl.semaphore_wait(barrier, len(partners))
     start_halos(warm_halos)
     tiles.start()
@@ -281,27 +280,29 @@
         mid[b * TILE : (b + 1) * TILE, :] = dot(inv[b], held[n])
         if n == 1:
             start_halos(mid_halos)
+    ids_now = ids_row.astype(jnp.int32)
+    group = IFACE // NEAR
+    index = lax.broadcasted_iota(jnp.int32, (group, rows), 0)
+
+    def index_target(target):
+        if not reduce_here:
+            return index + target * group
+        return (index // owned) * (NEAR * owned) + target * owned + lax.rem(index, owned)
+
+    def pick(target):
+        return jnp.where(index_target(target) == ids_now, 1.0, 0.0).astype(jnp.bfloat16)
+
+    chosen = [pick(lax.rem(lo + k, NEAR)) for k in range(NEAR)] if reduce_here else []
     for n, b in enumerate(order[2:] + order[:2]):
         if n == blocks - 2:
             wait_halos(1, mid_halos)
         part = pl.ds(b * TILE, TILE)
         modes_ref[part, :] = dot(inv[b], residual(b, old(mid, 1, b - 1), old(mid, 1, b + 1)))
 
-    ids_now = ids_row.astype(jnp.int32)
     weighted_high, weighted_low = split(values_col * modes_ref[...])
-    group = IFACE // NEAR
-    index = lax.broadcasted_iota(jnp.int32, (group, rows), 0)
-
-    def pick(target):
-        return jnp.where(index_target(target) == ids_now, 1.0, 0.0).astype(jnp.bfloat16)
 
     def share(chosen, part=slice(None)):
         return product(chosen, weighted_high[:, part]) + product(chosen, weighted_low[:, part])
-
-    def index_target(target):
-        if not reduce_here:
-            return index + target * group
-        return (index // owned) * (NEAR * owned) + target * owned + lax.rem(index, owned)
 
     if not reduce_here:
         for k in range(NEAR):
@@ -310,7 +311,6 @@
 
     half = width // 2
     halves = [slice(0, half), slice(half, width)]
-    chosen = [pick(lax.rem(lo + k, NEAR)) for k in range(NEAR)]
     near_sent = []
     for h, part in enumerate(halves):
         for k in range(1, NEAR):

time: 36.9 us -> 36.8 us (level)
  no operation moved by 1% of the time
where the time goes in v6:
time: 36.8 us; the launch traced here: 36.6 us
  Pallas kernels  34.6 us (94%)
  local copies, waits for them, and re-layouts  1.41 us (4%)
  between operations  0.64 us (2%)
    pallas_call x1, Pallas kernels, on_device(): pl.pallas_call(functools.partial(body, slabs, reduce_here), out_shape=(ja...  34.6 us
    unnamed x2, local copies, waits for them, and re-layouts  1.41 us

profile of v6, /device:TPU:0, one launch (start us, length us, event | category | flops | bytes accessed | tf_op | source)
XLA Modules:
  0.0 36.6 jit_solution(4497279549956881454)
XLA Ops:
  0.6 34.6 %shard_map.95 = (f32[512,256]{1,0:T(8,128)S(1)}, f32[32,256]{1,0:T(8,128)S(1)}) custom-call(s32[2,2]{1,0:T(2,128)} %pattern_ref.1, f32[2,128,128]{2,1,0:T(8,128)} %diagonal_hbm.1, f32[2,128,128]{2,1,0:T(8,128)} %lower_hbm.1, f32[2,128,128]{2,1,0:T(8,128)} %upper_hbm.1, s32[1,512]{1,0:T(1,128)} %bitcast.2, f32[1,512]{1,0:T(1,128)} %bitcast.3, ...), custom_call_target="tpu_custom_call" | custom-call | tf_op jit(solution)/shard_map/pallas_call | solution.py:374
  35.2 0.8 %copy.12 = f32[512,256]{1,0:T(8,128)} copy(f32[512,256]{1,0:T(8,128)S(1)} %get-tuple-element.4) | data formatting | bytes 1048576
  36.0 0.6 %copy.13 = f32[32,256]{1,0:T(8,128)} copy(f32[32,256]{1,0:T(8,128)S(1)} %get-tuple-element.5) | data formatting | bytes 65536
